TPU v7x, 128 devices: a whole 4x4x4 slice. The times are simulated.
128 devices in a mesh: grp: 4 (over y), shard: 32 (over x, z, core).
Axes of the slice: x: 4, y: 4, z: 4, core: 2. Of those that a mesh axis runs over, the one named last changes fastest.
Arguments:
- new_rows: bfloat16 [32768, 1024], P(('grp', 'shard'))
- cluster_ids: int32 [32768], P(('grp', 'shard')), may hold values from 0 to 7, as said below
- new_order: int32 [32768], P(('grp', 'shard')), may hold values from 0 to 2147483646
- codes: bfloat16 [8, 8192, 1024], P('grp', 'shard'), may hold values from -8 to 8
- scales: float32 [8, 1024], P('grp')
- offsets: float32 [8, 1024], P('grp')
- counts: int32 [8], P('grp'), may hold values from 1024 to 8192, as said below
- earlier_order: int32 [8, 8192], P('grp', 'shard'), may hold values from 1 to 2147483646
Outputs:
- max_similarity: float32 [32768], P(('grp', 'shard'))
Inputs may be any that keep to these rules, and one draw needn't show every extreme that they name: `cluster_ids`: in each device's block of 256 rows, no group's clusters are named by more than 128 rows, and some group's clusters are named by exactly 128 rows. `counts`: some cluster has all 8192 slots live.
All inputs are finite; a program needn't handle non-finite values.
Results may differ from a plain program's by a relative error of at most 0.00047.
Values may be sent and summed in bfloat16 or wider, within the bound.
A program may use at most 128 MiB of HBM per device.

v0:
```python
import jax
import jax.numpy as jnp
from jax import lax
from jax.sharding import PartitionSpec as P

epsilon = 1e-06


def unit_rows(values):
    return (values / jnp.sqrt(jnp.sum(values * values, axis=-1, keepdims=True) + epsilon)).astype(
        jnp.bfloat16
    )


def score_clusters(
    running, queries, query_cluster, query_order, key_source, key_order, live_counts, prepare
):
    width = key_source.shape[1]
    positions = jnp.arange(width, dtype=jnp.int32)
    best = running
    for cluster in range(key_source.shape[0]):
        cluster_keys = prepare(key_source[cluster], cluster)
        scores = jnp.dot(queries, cluster_keys.T, preferred_element_type=jnp.float32)
        allowed = (
            (query_cluster[:, None] == cluster)
            & (positions[None, :] < live_counts[cluster])
            & (key_order[cluster][None, :] < query_order[:, None])
        )
        best = jnp.maximum(best, jnp.max(jnp.where(allowed, scores, -1.0), axis=1))
    return best


def per_device(new_rows, cluster_ids, new_order, codes, scales, offsets, counts, earlier_order):
    groups = lax.axis_size("grp")
    owned_count = codes.shape[0]
    local_rows = new_rows.shape[0]
    capacity = local_rows // 2
    queries = unit_rows(new_rows.astype(jnp.float32))
    target = cluster_ids // owned_count
    onehot = (target[:, None] == jnp.arange(groups, dtype=jnp.int32)[None, :]).astype(jnp.int32)
    slot_rank = jnp.sum((jnp.cumsum(onehot, axis=0) - onehot) * onehot, axis=1)
    position = target * capacity + slot_rank
    received = groups * capacity
    matches = position[None, :] == jnp.arange(received, dtype=jnp.int32)[:, None]
    filled = jnp.any(matches, axis=1)
    source_row = jnp.sum(
        jnp.where(matches, jnp.arange(local_rows, dtype=jnp.int32)[None, :], 0), axis=1
    )
    send_rows = jnp.take(queries, source_row, axis=0).reshape(groups, capacity, queries.shape[1])
    send_cluster = jnp.where(filled, jnp.take(cluster_ids % owned_count, source_row), 0).reshape(
        groups, capacity
    )
    send_order = jnp.where(filled, jnp.take(new_order, source_row), 0).reshape(groups, capacity)
    got_rows, got_cluster, got_order = (
        lax.all_to_all(send_rows, "grp", split_axis=0, concat_axis=0, tiled=True),
        lax.all_to_all(send_cluster, "grp", split_axis=0, concat_axis=0, tiled=True),
        lax.all_to_all(send_order, "grp", split_axis=0, concat_axis=0, tiled=True),
    )
    got_rows = got_rows.reshape(received, queries.shape[1])
    got_cluster = got_cluster.reshape(received)
    got_order = got_order.reshape(received)
    starting = jnp.zeros((received,), jnp.float32)

    def decode_one(code_rows, cluster):
        return unit_rows(
            code_rows.astype(jnp.float32) * scales[cluster][None, :] + offsets[cluster][None, :]
        )

    top_score = score_clusters(
        starting,
        got_rows,
        got_cluster,
        got_order,
        lax.all_gather(codes, "shard", axis=1, tiled=True),
        lax.all_gather(earlier_order, "shard", axis=1, tiled=True),
        counts,
        decode_one,
    )
    answered = lax.all_to_all(
        top_score.reshape(groups, capacity), "grp", split_axis=0, concat_axis=0, tiled=True
    )
    return jnp.take(answered.reshape(received), position)


def solution(mesh):
    return jax.shard_map(
        per_device,
        mesh=mesh,
        in_specs=(
            P(("grp", "shard"), None),
            P(("grp", "shard")),
            P(("grp", "shard")),
            P("grp", "shard", None),
            P("grp", None),
            P("grp", None),
            P("grp"),
            P("grp", "shard"),
        ),
        out_specs=P(("grp", "shard")),
        check_vma=False,
    )
```

profile of v0, /device:TPU:0, one launch (start us, length us, event | category | flops | bytes accessed | tf_op | source)
XLA Modules:
  0.0 194.7 jit_solution(17353483784496994221)
XLA Ops:
  6.5 0.0 copy-start
  6.5 0.0 all-gather.2.cloned.1.call-start
  6.5 0.7 all-gather.2.cloned.1.call-update
  7.3 0.7 and_select_fusion
  8.0 1.2 reduce-window.6
  9.2 0.1 slice.56
  9.3 0.1 copy.15
  9.4 0.1 copy.16
  9.5 0.1 add_bitcast_fusion
  9.6 0.6 compare_select_fusion.3
  10.2 0.0 copy-start.1
  10.2 0.1 select_reduce_fusion.2
  10.3 3.5 %gather_fusion.2 = s32[512]{0:T(512)S(1)} fusion(s32[256]{0:T(256)S(1)} %get-tuple-element.20, s32[1024]{0:T(1024)S(1)} %pad_clamp_fusion.2), kind=kCustom, calls=%fused_computation.clone | custom fusion | bytes 6144 | tf_op jit(solution)/shard_map/jit(_take)/gather | solution.py:50
  13.9 0.0 copy-done
  13.9 3.5 %gather_fusion.3 = s32[512]{0:T(512)S(1)} fusion(s32[256]{0:T(256)S(1)} %copy-done, s32[1024]{0:T(1024)S(1)} %pad_clamp_fusion.2), kind=kCustom, calls=%fused_computation.1.clone | custom fusion | bytes 6144 | tf_op jit(solution)/shard_map/jit(_take)/gather | solution.py:53
  17.4 0.2 fusion.28
  17.6 0.5 select_select_fusion.1
  18.1 4.5 %all-to-all-start = ((s32[4,1,128]{2,1,0:T(1,128)}), s32[4,1,128]{2,1,0:T(1,128)S(1)}, u32[]{:S(2)}, u32[]{:S(2)}) async-start(s32[4,1,128]{2,1,0:T(1,128)} %bitcast.3), calls=%async_computation | async-start | bytes 4096 | tf_op jit(solution)/shard_map/all_to_all | solution.py:56
  22.7 1.3 fusion.26
  24.0 0.0 copy-done.1
  24.0 1.4 fusion.27
  25.3 2.1 %gather_fusion = bf16[512,1024]{1,0:T(8,128)(2,1)S(1)} fusion(bf16[256,1024]{1,0:T(8,128)(2,1)S(1)} %fusion.27, s32[1024]{0:T(1024)S(1)} %pad_clamp_fusion.1), kind=kCustom, calls=%fused_computation.2 | custom fusion | bytes 2099200 | tf_op jit(solution)/shard_map/jit(_take)/gather | solution.py:49
  27.4 25.5 %all_gather.6 = s32[2,8192]{1,0:T(2,128)S(1)} all-gather(s32[2,256]{1,0:T(2,128)} %param.17), channel_id=1, replica_groups=mesh['grp'=4,'shard'=32] {'shard'}, dimensions={1}, use_global_device_ids=true | all-gather | bytes 67584 | tf_op jit(solution)/shard_map/all_gather | solution.py:75
  52.9 1.3 fusion.35
  54.2 0.7 iota_compare_fusion.2
  54.9 0.8 fusion.33
  55.7 0.8 fusion.34
  56.5 1.2 broadcast_select_fusion
  57.6 0.1 fusion.32
  57.7 0.6 iota_compare_fusion.1
  58.2 0.0 all-to-all-done
  58.2 4.7 %all-to-all-start.1 = ((s32[4,1,128]{2,1,0:T(1,128)}), s32[4,1,128]{2,1,0:T(1,128)S(1)}, u32[]{:S(2)}, u32[]{:S(2)}) async-start(s32[4,1,128]{2,1,0:T(1,128)} %bitcast.6), calls=%async_computation.1 | async-start | bytes 4096 | tf_op jit(solution)/shard_map/all_to_all | solution.py:57
  63.0 5.2 %all-to-all-done.1 = s32[4,1,128]{2,1,0:T(1,128)S(1)} async-done(((s32[4,1,128]{2,1,0:T(1,128)}), s32[4,1,128]{2,1,0:T(1,128)S(1)}, u32[]{:S(2)}, u32[]{:S(2)}) %all-to-all-start.1) | async-done | bytes 2080 | tf_op jit(solution)/shard_map/all_to_all | solution.py:57
  68.2 3.5 %all-to-all-start.2 = ((bf16[4,128,1024]{2,1,0:T(8,128)(2,1)}), bf16[4,128,1024]{2,1,0:T(8,128)(2,1)S(1)}, u32[]{:S(2)}, u32[]{:S(2)}) async-start(bf16[4,128,1024]{2,1,0:T(8,128)(2,1)} %broadcast_select_fusion), calls=%async_computation.2 | async-start | bytes 2097152 | tf_op jit(solution)/shard_map/all_to_all | solution.py:55
  71.8 54.4 %all-gather.2.cloned.1.call-done = bf16[2,8192,1024]{2,1,0:T(8,128)(2,1)} async-done(((bf16[2,256,1024]{2,1,0:T(8,128)(2,1)}), bf16[2,8192,1024]{2,1,0:T(8,128)(2,1)}) %all-gather.2.cloned.1.call-update) | async-done | bytes 33554448 | tf_op jit(solution)/shard_map/all_gather | solution.py:74
  126.2 20.2 %fusion.6 = (f32[8192]{0:T(1024)S(1)}, f32[8192]{0:T(1024)S(1)}) fusion(f32[1024]{0:T(1024)S(1)} %bitcast.89, f32[1024]{0:T(1024)S(1)} %bitcast.87, bf16[2,8192,1024]{2,1,0:T(8,128)(2,1)} %all-gather.2.cloned.1.call-done, f32[1024]{0:T(1024)S(1)} %bitcast.85, f32[1024]{0:T(1024)S(1)} %bitcast.83), kind=kLoop, calls=%fused_computation.14 | loop fusion | flops 83869696 | bytes 33636352 | tf_op jit(solution)/shard_map/reduce_sum | solution.py:10
  146.4 0.0 all-to-all-done.2
  146.4 14.4 %select_reduce_fusion.1 = f32[512]{0:T(512)S(1)} fusion(s32[8192]{0:T(1024)S(1)} %bitcast.81, s32[512]{0:T(512)S(1)} %bitcast.93, pred[8192]{0:T(1024)(128)(4,1)S(1)} %iota_compare_fusion.2, pred[512]{0:T(512)(128)(4,1)S(1)} %bitcast.96, bf16[512,1024]{1,0:T(8,128)(2,1)S(1)} %bitcast.77, f32[8192]{0:T(1024)S(1)} %get-tuple-element.25, ...), kind=kOutput, calls=%fused_computation.25 | convolution fusion | flops 8652849152 | bytes 17912320 | tf_op jit(solution)/shard_map/dot_general | solution.py:23
  160.8 0.0 copy-start.3
  160.8 0.0 copy-start.2
  160.9 14.5 %select_reduce_fusion = f32[512]{0:T(512)S(1)} fusion(s32[8192]{0:T(1024)S(1)} %bitcast.80, s32[512]{0:T(512)S(1)} %bitcast.94, pred[8192]{0:T(1024)(128)(4,1)S(1)} %iota_compare_fusion.1, pred[512]{0:T(512)(128)(4,1)S(1)} %bitcast.95, bf16[512,1024]{1,0:T(8,128)(2,1)S(1)} %bitcast.78, f32[8192]{0:T(1024)S(1)} %get-tuple-element.24, f32[1024]{0:T(1024)S(1)} %bitcast.86, ...), kind=kOutput, calls=%fused_computation.24 | convolution fusion | flops 8652849152 | bytes 17912320 | tf_op jit(solution)/shard_map/dot_general | solution.py:23
  175.3 0.6 maximum_maximum_fusion
  175.9 4.3 %all-to-all-start.3 = ((f32[4,1,128]{2,1,0:T(1,128)}), f32[4,1,128]{2,1,0:T(1,128)S(1)}, u32[]{:S(2)}, u32[]{:S(2)}) async-start(f32[4,1,128]{2,1,0:T(1,128)} %bitcast.23), calls=%async_computation.3 | async-start | bytes 4096 | tf_op jit(solution)/shard_map/all_to_all | solution.py:79
  180.2 0.0 copy-done.3
  180.2 5.1 %all-to-all-done.3 = f32[4,1,128]{2,1,0:T(1,128)S(1)} async-done(((f32[4,1,128]{2,1,0:T(1,128)}), f32[4,1,128]{2,1,0:T(1,128)S(1)}, u32[]{:S(2)}, u32[]{:S(2)}) %all-to-all-start.3) | async-done | bytes 2080 | tf_op jit(solution)/shard_map/all_to_all | solution.py:79
  185.3 1.9 gather_fusion.1
  187.3 0.0 copy-done.2
  187.3 0.6 and_select_fusion.1
  (13 shorter events, 0.2 us)
Async XLA Ops:
  6.5 7.3 %copy-start = (s32[256]{0:T(256)S(1)}, s32[256]{0:T(256)}, u32[]{:S(2)}) copy-start(s32[256]{0:T(256)} %param.12) | copy-start | bytes 3076
  6.5 119.7 %all-gather.2.cloned.1.call-start = ((), (), s32[]{:S(2)}) async-start(), calls=%async_computation.4 | async-start | bytes 34603008 | tf_op jit(solution)/shard_map/all_gather | solution.py:74
  10.2 13.8 %copy-start.1 = (s32[256]{0:T(256)}, s32[256]{0:T(256)S(1)}, u32[]{:S(2)}) copy-start(s32[256]{0:T(256)S(1)} %get-tuple-element.11) | copy-start | bytes 3076
  18.1 40.1 %all-to-all-start = ((s32[4,1,128]{2,1,0:T(1,128)}), s32[4,1,128]{2,1,0:T(1,128)S(1)}, u32[]{:S(2)}, u32[]{:S(2)}) async-start(s32[4,1,128]{2,1,0:T(1,128)} %bitcast.3), calls=%async_computation | async-start | bytes 4096 | tf_op jit(solution)/shard_map/all_to_all | solution.py:56
  58.2 10.0 %all-to-all-start.1 = ((s32[4,1,128]{2,1,0:T(1,128)}), s32[4,1,128]{2,1,0:T(1,128)S(1)}, u32[]{:S(2)}, u32[]{:S(2)}) async-start(s32[4,1,128]{2,1,0:T(1,128)} %bitcast.6), calls=%async_computation.1 | async-start | bytes 4096 | tf_op jit(solution)/shard_map/all_to_all | solution.py:57
  68.2 78.2 %all-to-all-start.2 = ((bf16[4,128,1024]{2,1,0:T(8,128)(2,1)}), bf16[4,128,1024]{2,1,0:T(8,128)(2,1)S(1)}, u32[]{:S(2)}, u32[]{:S(2)}) async-start(bf16[4,128,1024]{2,1,0:T(8,128)(2,1)} %broadcast_select_fusion), calls=%async_computation.2 | async-start | bytes 2097152 | tf_op jit(solution)/shard_map/all_to_all | solution.py:55
  160.8 19.4 %copy-start.3 = (s32[256]{0:T(256)S(1)}, s32[256]{0:T(256)}, u32[]{:S(2)}) copy-start(s32[256]{0:T(256)} %get-tuple-element.10) | copy-start | bytes 3076
  160.8 26.4 %copy-start.2 = (s32[256]{0:T(256)S(1)}, s32[256]{0:T(256)}, u32[]{:S(2)}) copy-start(s32[256]{0:T(256)} %copy-done.1) | copy-start | bytes 3076
  175.9 9.4 %all-to-all-start.3 = ((f32[4,1,128]{2,1,0:T(1,128)}), f32[4,1,128]{2,1,0:T(1,128)S(1)}, u32[]{:S(2)}, u32[]{:S(2)}) async-start(f32[4,1,128]{2,1,0:T(1,128)} %bitcast.23), calls=%async_computation.3 | async-start | bytes 4096 | tf_op jit(solution)/shard_map/all_to_all | solution.py:79
Sparse Core Ops, SparseCore 0:
  9.7 116.4 all-gather.1
where the time goes:
time: 195 us
  waiting for transfers between devices  65.5 us (34%)
  other arithmetic  29.9 us (15%)
  matrix products  28.9 us (15%)
  blocking collectives  25.5 us (13%)
  starting transfers between devices  17.1 us (9%)
  local copies, waits for them, and re-layouts  14.3 us (7%)
  between operations  13.6 us (7%)
    all_gather x1, waiting for transfers between devices, per_device(): lax.all_gather(codes, 'shard', axis=1, tiled=True)  54.4 us
    dot_general x2, matrix products, score_clusters(): jnp.dot(queries, cluster_keys.T, preferred_element_type=jnp.float32)  28.9 us
    all_gather x1, blocking collectives, per_device(): lax.all_gather(earlier_order, 'shard', axis=1, tiled=True)  25.5 us
    reduce_sum x2, other arithmetic, unit_rows(): jnp.sum(values * values, axis=-1, keepdims=True) + epsilon  21.4 us
    all_to_all x1, waiting for transfers between devices, per_device(): lax.all_to_all(send_order, 'grp', split_axis=0, concat_axis=0, tiled=True)  5.23 us
    all_to_all x1, waiting for transfers between devices, per_device(): lax.all_to_all(top_score.reshape(groups, capacity), 'grp', split_axis=0,...  5.09 us
    all_to_all x1, starting transfers between devices, per_device(): lax.all_to_all(send_order, 'grp', split_axis=0, concat_axis=0, tiled=True)  4.72 us
    all_to_all x1, starting transfers between devices, per_device(): lax.all_to_all(send_cluster, 'grp', split_axis=0, concat_axis=0, tiled=True)  4.55 us
  transfers between devices with their start and end apart: 5, of which 3 were waited for; matrix products, arithmetic and copies ran while one was open for 21% of the time, Pallas kernels for 0%

commit v1 on v0

--- a/solution.py
+++ b/solution.py
@@ -4,6 +4,28 @@
 from jax.sharding import PartitionSpec as P
 
 epsilon = 1e-06
+
+
+def in_order(blocks, dim):
+    blocks = jnp.moveaxis(blocks, 0, dim)
+    shape = blocks.shape
+    return blocks.reshape(*shape[:dim], shape[dim] * shape[dim + 1], *shape[dim + 2 :])
+
+
+def grow_blocks(array, axis):
+    length = lax.axis_size(axis)
+    blocks = array[None]
+    for level in range(length.bit_length() - 1):
+        bit = 1 << level
+        other = lax.ppermute(blocks, axis, [(i, i ^ bit) for i in range(length)])
+        both = jnp.stack([blocks, other])
+        upper = lax.axis_index(axis) >> level & 1
+        blocks = jnp.where(upper == 0, both, both[::-1]).reshape(-1, *array.shape)
+    return blocks
+
+
+def doubled_up(x, axis, dim):
+    return in_order(grow_blocks(x, axis), dim)
 
 
 def unit_rows(values):
@@ -71,7 +93,7 @@
         got_rows,
         got_cluster,
         got_order,
-        lax.all_gather(codes, "shard", axis=1, tiled=True),
+        doubled_up(codes, "shard", 1),
         lax.all_gather(earlier_order, "shard", axis=1, tiled=True),
         counts,
         decode_one,

time: 195 us -> 913 us (4.68)
  blocking collectives: 25.5 us -> 360 us
  waiting for transfers between devices: 65.5 us -> 324 us
  other arithmetic: 29.9 us -> 159 us
  between operations: 13.6 us -> 0.3 us
  starting transfers between devices: 17.1 us -> 28.8 us
    all_gather x1, blocking collectives: 25.5 us -> 360 us  [per_device(): lax.all_gather(earlier_order, 'shard', axis=1, tiled=True)]
    ppermute x0 -> x5, waiting for transfers between devices: none -> 319 us  [grow_blocks(): other = lax.ppermute(blocks, axis, [(i, i ^ bit) for i in range(length)])]
    select_n x0 -> x4, other arithmetic: none -> 60.6 us  [grow_blocks(): blocks = jnp.where(upper == 0, both, both[::-1]).reshape(-1, *array.shape)]
    all_gather x1 -> x0, waiting for transfers between devices: 54.4 us -> none  [per_device(): lax.all_gather(codes, 'shard', axis=1, tiled=True)]
    another operation x2 -> x8, other arithmetic: 1.26 us -> 44.9 us  [the longest x6 43.7 us: grow_blocks(): both = jnp.stack([blocks, other])]
    convert_element_type x1 -> x2, other arithmetic: 1.36 us -> 28.6 us  [unit_rows(): (values / jnp.sqrt(jnp.sum(values * values, axis=-1, keepdims=True) + eps...]
    ppermute x0 -> x5, starting transfers between devices: none -> 10.2 us  [grow_blocks(): other = lax.ppermute(blocks, axis, [(i, i ^ bit) for i in range(length)])]
  transfers between devices with their start and end apart: 5 -> 9, of which waited for: 3 -> 5; matrix products, arithmetic and copies ran while one was open for 21% -> 13% of each run, Pallas kernels for 0% -> 0%
where the time goes in v1:
time: 913 us; the launch traced here: 912 us
  blocking collectives  360 us (39%)
  waiting for transfers between devices  324 us (35%)
  other arithmetic  159 us (17%)
  starting transfers between devices  28.8 us (3%)
  matrix products  27.3 us (3%)
  local copies, waits for them, and re-layouts  12 us (1%)
    all_gather x1, blocking collectives, per_device(): lax.all_gather(earlier_order, 'shard', axis=1, tiled=True)  360 us
    ppermute x5, waiting for transfers between devices, grow_blocks(): other = lax.ppermute(blocks, axis, [(i, i ^ bit) for i in range(length)])  319 us
    select_n x4, other arithmetic, grow_blocks(): blocks = jnp.where(upper == 0, both, both[::-1]).reshape(-1, *array.shape)  60.6 us
    another operation x6, other arithmetic, grow_blocks(): both = jnp.stack([blocks, other])  43.7 us
    convert_element_type x2, other arithmetic, unit_rows(): (values / jnp.sqrt(jnp.sum(values * values, axis=-1, keepdims=True) + eps...  28.6 us
    dot_general x2, matrix products, score_clusters(): jnp.dot(queries, cluster_keys.T, preferred_element_type=jnp.float32)  27.3 us
    reduce_sum x2, other arithmetic, unit_rows(): jnp.sum(values * values, axis=-1, keepdims=True) + epsilon  20.5 us
  transfers between devices with their start and end apart: 9, of which 5 were waited for; matrix products, arithmetic and copies ran while one was open for 13% of the time, Pallas kernels for 0%

profile of v1, /device:TPU:0, one launch (start us, length us, event | category | flops | bytes accessed | tf_op | source)
XLA Modules:
  0.0 912.1 jit_solution(12397598160608921297)
XLA Ops:
  0.0 0.0 collective-permute-start
  0.0 2.9 collective-permute-done
  2.9 1.4 pad_maximum_fusion.4
  4.3 2.2 fusion.1
  6.5 2.0 collective-permute-start.1
  8.5 46.2 %collective-permute-done.1 = bf16[2,2,256,1024]{3,2,1,0:T(8,128)(2,1)} collective-permute-done((bf16[2,2,256,1024]{3,2,1,0:T(8,128)(2,1)}, bf16[2,2,256,1024]{3,2,1,0:T(8,128)(2,1)}, u32[]{:S(2)}, u32[]{:S(2)}) %collective-permute-start.1) | collective-permute-done | bytes 2097184 | tf_op jit(solution)/shard_map/ppermute | solution.py:20
  54.7 2.0 pad_maximum_fusion.3
  56.7 3.2 reverse_select_fusion.3
  59.9 3.7 collective-permute-start.2
  63.6 90.4 %collective-permute-done.2 = bf16[4,2,256,1024]{3,2,1,0:T(8,128)(2,1)} collective-permute-done((bf16[4,2,256,1024]{3,2,1,0:T(8,128)(2,1)}, bf16[4,2,256,1024]{3,2,1,0:T(8,128)(2,1)}, u32[]{:S(2)}, u32[]{:S(2)}) %collective-permute-start.2) | collective-permute-done | bytes 4194336 | tf_op jit(solution)/shard_map/ppermute | solution.py:20
  154.0 7.5 pad_maximum_fusion.2
  161.5 13.6 %reverse_select_fusion.2 = bf16[2,4,2,256,1024]{4,3,2,1,0:T(8,128)(2,1)} fusion(bf16[2,4,2,256,1024]{4,3,2,1,0:T(8,128)(2,1)} %pad_maximum_fusion.2, pred[]{:T(512)S(6)} %eq.96), kind=kLoop, calls=%fused_computation.16 | loop fusion | flops 4194304 | bytes 16777216 | tf_op jit(solution)/shard_map/jit(_where)/select_n | solution.py:23
  175.0 1.5 collective-permute-start.3
  176.5 179.9 %collective-permute-done.3 = bf16[8,2,256,1024]{3,2,1,0:T(8,128)(2,1)} collective-permute-done((bf16[8,2,256,1024]{3,2,1,0:T(8,128)(2,1)}, bf16[8,2,256,1024]{3,2,1,0:T(8,128)(2,1)}, u32[]{:S(2)}, u32[]{:S(2)}) %collective-permute-start.3) | collective-permute-done | bytes 8388640 | tf_op jit(solution)/shard_map/ppermute | solution.py:20
  356.4 8.0 pad_maximum_fusion.1
  364.4 0.0 copy-start.7
  364.4 0.0 copy-start.2
  364.4 0.0 copy-start.5
  364.4 0.0 copy-start.6
  364.5 0.0 copy-start.3
  364.5 0.0 copy-start.4
  364.5 10.5 %reverse_select_fusion.1 = bf16[2,8,2,256,1024]{4,3,2,1,0:T(8,128)(2,1)} fusion(bf16[2,8,2,256,1024]{4,3,2,1,0:T(8,128)(2,1)S(1)} %pad_maximum_fusion.1, pred[]{:T(512)S(6)} %eq.95), kind=kLoop, calls=%fused_computation.12 | loop fusion | flops 8388608 | bytes 33554432 | tf_op jit(solution)/shard_map/jit(_where)/select_n | solution.py:23
  375.0 3.0 collective-permute-start.4
  378.0 1.2 reduce-window.6
  379.3 0.1 slice.58
  379.3 0.1 copy.15
  379.5 0.1 copy.16
  379.6 0.1 add_bitcast_fusion
  379.7 0.2 select_reduce_fusion.2
  379.9 3.5 gather_fusion.2
  383.4 0.0 copy-done
  383.4 3.5 gather_fusion.3
  386.9 0.2 fusion.4
  387.1 0.6 select_select_fusion.1
  387.7 4.5 all-to-all-start
  392.2 0.2 fusion.2
  392.4 0.2 fusion.3
  392.6 2.1 gather_fusion
  394.7 0.0 copy-done.5
  394.7 359.8 %all_gather.3 = s32[2,8192]{1,0:T(2,128)S(1)} all-gather(s32[2,256]{1,0:T(2,128)S(1)} %copy-done.5), channel_id=1, replica_groups=mesh['grp'=4,'shard'=32] {'shard'}, dimensions={1}, use_global_device_ids=true | all-gather | bytes 67584 | tf_op jit(solution)/shard_map/all_gather | solution.py:97
  754.5 0.6 fusion.11
  755.1 0.7 iota_compare_fusion.2
  755.8 0.0 copy-done.4
  755.9 1.1 broadcast_select_fusion
  757.0 0.1 fusion.8
  757.1 0.6 iota_compare_fusion.1
  757.7 0.0 all-to-all-done
  757.7 4.5 all-to-all-start.1
  762.2 0.0 collective-permute-done.4
  762.2 22.6 %pad_maximum_fusion = bf16[2,16,2,256,1024]{4,3,2,1,0:T(8,128)(2,1)} fusion(bf16[1,16,2,256,1024]{4,3,2,1,0:T(8,128)(2,1)} %bitcast.27, bf16[1,16,2,256,1024]{4,3,2,1,0:T(8,128)(2,1)} %bitcast.25), kind=kLoop, calls=%fused_computation.5 | loop fusion | flops 16777216 | bytes 67108864 | tf_op jit(solution)/shard_map/stack | solution.py:21
  784.8 33.3 %reverse_select_fusion = bf16[2,16,2,256,1024]{4,3,2,1,0:T(8,128)(2,1)} fusion(bf16[2,16,2,256,1024]{4,3,2,1,0:T(8,128)(2,1)} %pad_maximum_fusion, pred[]{:T(512)S(6)} %eq.94), kind=kLoop, calls=%fused_computation.4 | loop fusion | flops 16777216 | bytes 67108864 | tf_op jit(solution)/shard_map/jit(_where)/select_n | solution.py:23
  818.2 20.3 %multiply_reduce_fusion.1 = (f32[32,256]{1,0:T(8,128)S(1)}, f32[32,256]{1,0:T(8,128)S(1)}) fusion(f32[1024]{0:T(1024)S(1)} %bitcast.89, f32[1024]{0:T(1024)S(1)} %bitcast.85, bf16[2,32,256,1024]{3,2,0,1:T(8,128)(2,1)} %bitcast.70, f32[1024]{0:T(1024)S(1)} %bitcast.87, f32[1024]{0:T(1024)S(1)} %bitcast.83), kind=kLoop, calls=%fused_computation.10 | loop fusion | flops 83869696 | bytes 33636352 | tf_op jit(solution)/shard_map/reduce_sum | solution.py:32
  838.5 0.0 all-to-all-done.1
  838.5 4.8 all-to-all-start.2
  843.3 28.4 %divide_convert_fusion.1 = (bf16[1,32,256,1024]{3,2,0,1:T(8,128)(2,1)}, bf16[1,32,256,1024]{3,2,0,1:T(8,128)(2,1)}) fusion(f32[32,256]{1,0:T(8,128)S(1)} %get-tuple-element.29, f32[1024]{0:T(1024)S(1)} %bitcast.90, f32[1024]{0:T(1024)S(1)} %bitcast.86, bf16[2,32,256,1024]{3,2,0,1:T(8,128)(2,1)} %bitcast.71, f32[32,256]{1,0:T(8,128)S(1)} %get-tuple-element.28, ...), kind=kLoop, calls=%fused_computation.9 | loop fusion | flops 83886080 | bytes 67190784 | tf_op jit(solution)/shard_map/convert_element_type | solution.py:32
  871.8 0.0 all-to-all-done.2
  871.8 13.6 %select_reduce_fusion.1 = f32[512]{0:T(512)S(1)} fusion(bf16[512,1024]{1,0:T(8,128)(2,1)S(1)} %bitcast.77, bf16[8192,1024]{1,0:T(8,128)(2,1)} %bitcast.75, s32[8192]{0:T(1024)S(1)} %bitcast.92, s32[512]{0:T(512)S(1)} %bitcast.96, pred[8192]{0:T(1024)(128)(4,1)S(1)} %iota_compare_fusion.2, pred[512]{0:T(512)(128)(4,1)S(1)} %bitcast.99), kind=kOutput, calls=%fused_computation.15 | convolution fusion | flops 8610906112 | bytes 17871360 | tf_op jit(solution)/shard_map/dot_general | solution.py:45
  885.4 0.0 copy-start.1
  885.4 13.7 %select_reduce_fusion = f32[512]{0:T(512)S(1)} fusion(bf16[512,1024]{1,0:T(8,128)(2,1)S(1)} %bitcast.78, bf16[8192,1024]{1,0:T(8,128)(2,1)} %bitcast.74, s32[8192]{0:T(1024)S(1)} %bitcast.91, s32[512]{0:T(512)S(1)} %bitcast.97, pred[8192]{0:T(1024)(128)(4,1)S(1)} %iota_compare_fusion.1, pred[512]{0:T(512)(128)(4,1)S(1)} %bitcast.98), kind=kOutput, calls=%fused_computation.14 | convolution fusion | flops 8610906112 | bytes 17871360 | tf_op jit(solution)/shard_map/dot_general | solution.py:45
  899.1 0.6 maximum_maximum_fusion
  899.7 4.8 all-to-all-start.3
  904.5 5.1 all-to-all-done.3
  909.6 1.9 gather_fusion.1
  911.6 0.6 and_select_fusion.1
  (23 shorter events, 0.2 us)
Async XLA Ops:
  0.0 383.4 %copy-start = (s32[256]{0:T(256)S(1)}, s32[256]{0:T(256)}, u32[]{:S(2)}) copy-start(s32[256]{0:T(256)} %param.12) | copy-start | bytes 3076
  0.0 2.9 collective-permute-start
  6.5 48.2 %collective-permute-start.1 = (bf16[2,2,256,1024]{3,2,1,0:T(8,128)(2,1)}, bf16[2,2,256,1024]{3,2,1,0:T(8,128)(2,1)}, u32[]{:S(2)}, u32[]{:S(2)}) collective-permute-start(bf16[2,2,256,1024]{3,2,1,0:T(8,128)(2,1)} %get-tuple-element.15), channel_id=1, source_target_pairs={{0,2},{1,3},{2,0},{3,1},{4,6},{5,7},{6,4},{7,5},{8,10},{9,11},{10,... | collective-permute-start | bytes 6291464 | tf_op jit(solution)/shard_map/ppermute | solution.py:20
  59.9 94.1 %collective-permute-start.2 = (bf16[4,2,256,1024]{3,2,1,0:T(8,128)(2,1)}, bf16[4,2,256,1024]{3,2,1,0:T(8,128)(2,1)}, u32[]{:S(2)}, u32[]{:S(2)}) collective-permute-start(bf16[4,2,256,1024]{3,2,1,0:T(8,128)(2,1)} %bitcast.20), channel_id=1, source_target_pairs={{0,4},{1,5},{2,6},{3,7},{4,0},{5,1},{6,2},{7,3},{8,12},{9,13},{10,... | collective-permute-start | bytes 12582920 | tf_op jit(solution)/shard_map/ppermute | solution.py:20
  175.0 181.4 %collective-permute-start.3 = (bf16[8,2,256,1024]{3,2,1,0:T(8,128)(2,1)}, bf16[8,2,256,1024]{3,2,1,0:T(8,128)(2,1)}, u32[]{:S(2)}, u32[]{:S(2)}) collective-permute-start(bf16[8,2,256,1024]{3,2,1,0:T(8,128)(2,1)} %bitcast.72), channel_id=1, source_target_pairs={{0,8},{1,9},{2,10},{3,11},{4,12},{5,13},{6,14},{7,15},{8,0},{9,1},... | collective-permute-start | bytes 25165832 | tf_op jit(solution)/shard_map/ppermute | solution.py:20
  364.4 13.6 %copy-start.7 = (s32[256]{0:T(256)S(1)}, s32[256]{0:T(256)}, u32[]{:S(2)}) copy-start(s32[256]{0:T(256)} %param.11) | copy-start | bytes 3076
  364.4 27.8 %copy-start.2 = (bf16[256,1024]{1,0:T(8,128)(2,1)S(1)}, bf16[256,1024]{1,0:T(8,128)(2,1)}, u32[]{:S(2)}) copy-start(bf16[256,1024]{1,0:T(8,128)(2,1)} %param.10) | copy-start | bytes 1572868
  364.4 30.2 %copy-start.5 = (s32[2,256]{1,0:T(2,128)S(1)}, s32[2,256]{1,0:T(2,128)}, u32[]{:S(2)}) copy-start(s32[2,256]{1,0:T(2,128)} %param.17) | copy-start | bytes 6148
  364.4 390.1 %copy-start.6 = (s32[2]{0:T(128)S(1)}, s32[2]{0:T(128)}, u32[]{:S(2)}) copy-start(s32[2]{0:T(128)} %param.16) | copy-start | bytes 28
  364.5 391.4 %copy-start.3 = (f32[2,1024]{1,0:T(2,128)S(1)}, f32[2,1024]{1,0:T(2,128)}, u32[]{:S(2)}) copy-start(f32[2,1024]{1,0:T(2,128)} %param.14) | copy-start | bytes 24580
  364.5 391.4 %copy-start.4 = (f32[2,1024]{1,0:T(2,128)S(1)}, f32[2,1024]{1,0:T(2,128)}, u32[]{:S(2)}) copy-start(f32[2,1024]{1,0:T(2,128)} %param.15) | copy-start | bytes 24580
  375.0 387.2 %collective-permute-start.4 = (bf16[16,2,256,1024]{3,2,1,0:T(8,128)(2,1)}, bf16[16,2,256,1024]{3,2,1,0:T(8,128)(2,1)}, u32[]{:S(2)}, u32[]{:S(2)}) collective-permute-start(bf16[16,2,256,1024]{3,2,1,0:T(8,128)(2,1)} %bitcast.26), channel_id=1, source_target_pairs={{0,16},{1,17},{2,18},{3,19},{4,20},{5,21},{6,22},{7,23},{8,24},{9,... | collective-permute-start | bytes 50331656 | tf_op jit(solution)/shard_map/ppermute | solution.py:20
  387.7 370.0 %all-to-all-start = ((s32[4,1,128]{2,1,0:T(1,128)}), s32[4,1,128]{2,1,0:T(1,128)S(1)}, u32[]{:S(2)}, u32[]{:S(2)}) async-start(s32[4,1,128]{2,1,0:T(1,128)} %bitcast.3), calls=%async_computation | async-start | bytes 4096 | tf_op jit(solution)/shard_map/all_to_all | solution.py:78
  757.7 80.8 %all-to-all-start.1 = ((s32[4,1,128]{2,1,0:T(1,128)}), s32[4,1,128]{2,1,0:T(1,128)S(1)}, u32[]{:S(2)}, u32[]{:S(2)}) async-start(s32[4,1,128]{2,1,0:T(1,128)} %bitcast.6), calls=%async_computation.1 | async-start | bytes 4096 | tf_op jit(solution)/shard_map/all_to_all | solution.py:79
  838.5 33.2 %all-to-all-start.2 = ((bf16[4,128,1024]{2,1,0:T(8,128)(2,1)}), bf16[4,128,1024]{2,1,0:T(8,128)(2,1)S(1)}, u32[]{:S(2)}, u32[]{:S(2)}) async-start(bf16[4,128,1024]{2,1,0:T(8,128)(2,1)} %broadcast_select_fusion), calls=%async_computation.2 | async-start | bytes 2097152 | tf_op jit(solution)/shard_map/all_to_all | solution.py:77
  885.4 26.7 %copy-start.1 = (s32[256]{0:T(256)S(1)}, s32[256]{0:T(256)}, u32[]{:S(2)}) copy-start(s32[256]{0:T(256)} %param.12) | copy-start | bytes 3076
  899.7 9.9 %all-to-all-start.3 = ((f32[4,1,128]{2,1,0:T(1,128)}), f32[4,1,128]{2,1,0:T(1,128)S(1)}, u32[]{:S(2)}, u32[]{:S(2)}) async-start(f32[4,1,128]{2,1,0:T(1,128)} %bitcast.39), calls=%async_computation.3 | async-start | bytes 4096 | tf_op jit(solution)/shard_map/all_to_all | solution.py:101
